TPU v7x, 1024 devices: a whole 8x8x8 slice. The times are simulated.
1024 devices in a mesh: blk: 256 (over x, y_lo, z, core), grp: 4 (over y_hi).
Axes of the slice: x: 8, y: 8 (y_hi: 4, y_lo: 2; y = y_hi * 2 + y_lo), z: 8, core: 2. Of those that a mesh axis runs over, the one named last changes fastest.
Arguments:
- images: bfloat16 [131072, 1152], P(('blk', 'grp')), may hold values from -6 to 6
- texts: bfloat16 [131072, 1152], P(('blk', 'grp')), may hold values from -6 to 6
- scale: float32 [1], replicated, may hold values from 0.02 to 0.08
- bias: float32 [1], replicated, may hold values from -4 to -1
Outputs:
- loss_rows: float32 [131072], P(('blk', 'grp'))
- grad_images: float32 [131072, 1152], P(('blk', 'grp'))
- grad_texts: float32 [131072, 1152], P(('blk', 'grp'))
All inputs are finite; a program needn't handle non-finite values.
Results may differ from a plain program's by a relative error of at most 0.0023.
Values may be sent and summed in bfloat16 or wider, within the bound.
A program may use at most 32 MiB of HBM per device.

v0:
```python
import jax
import jax.numpy as jnp
from jax import lax
from jax.sharding import PartitionSpec as P

STEPS = 8


def shifted(value, axis, steps):
    count = lax.axis_size(axis)
    pairs = [(source, (source + steps) % count) for source in range(count)]
    return lax.ppermute(value, axis, pairs)


def tile_coef(images, partner, scale, bias, positive):
    logits = (
        scale[0]
        * lax.dot_general(
            images, partner, (((1,), (1,)), ((), ())), preferred_element_type=jnp.float32
        )
        + bias[0]
    )
    rows = images.shape[0]
    diagonal = lax.broadcasted_iota(jnp.int32, (rows, rows), 0) == lax.broadcasted_iota(
        jnp.int32, (rows, rows), 1
    )
    if positive:
        sign = jnp.where(diagonal, 1.0, -1.0).astype(jnp.float32)
    else:
        sign = -jnp.ones((rows, rows), jnp.float32)
    coef = (-sign * jax.nn.sigmoid(-sign * logits)).astype(jnp.bfloat16)
    return (logits, sign, coef)


def pair_block(images, partner, scale, bias, positive):
    logits, sign, coef = tile_coef(images, partner, scale, bias, positive)
    loss = jnp.sum(-jax.nn.log_sigmoid(sign * logits), axis=1)
    grad_img = jnp.dot(coef, partner, preferred_element_type=jnp.float32)
    return (loss, coef, grad_img)


def text_term(coef, images):
    return lax.dot_general(
        coef, images, (((0,), (0,)), ((), ())), preferred_element_type=jnp.float32
    )


def next_block(partner):
    return shifted(partner, "blk", 1)


def on_device(images, texts, scale, bias):
    cross = shifted(texts, "grp", 1)
    loss_total, coef, grad_img = pair_block(images, cross, scale, bias, False)
    cross_grad = shifted(text_term(coef, images), "grp", -1)
    partner = texts
    partial_value = jnp.zeros(images.shape, jnp.float32)
    for step in range(STEPS):
        if step > 0:
            partner = next_block(partner)
            partial_value = shifted(partial_value, "blk", 1)
        loss, coef, g_img = pair_block(images, partner, scale, bias, step == 0)
        loss_total = loss_total + loss
        grad_img = grad_img + g_img
        partial_value = partial_value + text_term(coef, images)
    own_grad = shifted(partial_value, "blk", -(STEPS - 1))
    grad_txt = scale[0] * (own_grad + cross_grad)
    return (loss_total, scale[0] * grad_img, grad_txt)


def solution(mesh):
    placed = (P(("blk", "grp"), None), P(("blk", "grp"), None), P(), P())
    return jax.shard_map(
        on_device,
        mesh=mesh,
        in_specs=placed,
        out_specs=(P(("blk", "grp")), P(("blk", "grp"), None), P(("blk", "grp"), None)),
        check_vma=False,
    )
```

profile of v0, /device:TPU:414, one launch (start us, length us, event | category | flops | bytes accessed | tf_op | source)
XLA Modules:
  0.0 159.6 jit_solution(589642185052507283)
XLA Ops:
  0.6 2.1 %collective-permute-start.1 = (bf16[128,1152]{1,0:T(8,128)(2,1)}, bf16[128,1152]{1,0:T(8,128)(2,1)S(1)}, u32[]{:S(2)}, u32[]{:S(2)}) collective-permute-start(bf16[128,1152]{1,0:T(8,128)(2,1)} %param.5), channel_id=1, source_target_pairs={{0,4},{4,8},{8,12},{12,16},{16,20},{20,24},{24,28},{28,32},{32,36}... | collective-permute-start | bytes 884744 | tf_op jit(solution)/shard_map/ppermute | solution.py:12
  2.7 4.7 %collective-permute-start = (bf16[128,1152]{1,0:T(8,128)(2,1)}, bf16[128,1152]{1,0:T(8,128)(2,1)S(1)}, u32[]{:S(2)}, u32[]{:S(2)}) collective-permute-start(bf16[128,1152]{1,0:T(8,128)(2,1)} %param.5), channel_id=1, source_target_pairs={{0,1},{1,2},{2,3},{3,0},{4,5},{5,6},{6,7},{7,4},{8,9},{9,10},{10,1... | collective-permute-start | bytes 884744 | tf_op jit(solution)/shard_map/ppermute | solution.py:12
  8.7 1.3 fusion.19
  10.0 0.2 fusion.36
  10.3 6.2 %collective-permute-start.8 = (f32[128,1152]{1,0:T(8,128)S(1)}, f32[128,1152]{1,0:T(8,128)S(1)}, u32[]{:S(2)}, u32[]{:S(2)}) collective-permute-start(f32[128,1152]{1,0:T(8,128)S(1)} %fusion.36), channel_id=1, source_target_pairs={{0,4},{4,8},{8,12},{12,16},{16,20},{20,24},{24,28},{28,32},{32,36}... | collective-permute-start | bytes 1769480 | tf_op jit(solution)/shard_map/ppermute | solution.py:12
  16.5 0.3 fusion.38
  16.8 4.9 %collective-permute-done = bf16[128,1152]{1,0:T(8,128)(2,1)S(1)} collective-permute-done((bf16[128,1152]{1,0:T(8,128)(2,1)}, bf16[128,1152]{1,0:T(8,128)(2,1)S(1)}, u32[]{:S(2)}, u32[]{:S(2)}) %collective-permute-start) | collective-permute-done | bytes 294944 | tf_op jit(solution)/shard_map/ppermute | solution.py:12
  21.7 0.3 fusion.18
  22.0 0.2 fusion.28
  22.2 4.4 %collective-permute-start.16 = (f32[128,1152]{1,0:T(8,128)S(1)}, f32[128,1152]{1,0:T(8,128)S(1)}, u32[]{:S(2)}, u32[]{:S(2)}) collective-permute-start(f32[128,1152]{1,0:T(8,128)S(1)} %fusion.28), channel_id=1, source_target_pairs={{0,3},{1,0},{2,1},{3,2},{4,7},{5,4},{6,5},{7,6},{8,11},{9,8},{10,9... | collective-permute-start | bytes 1769480 | tf_op jit(solution)/shard_map/ppermute | solution.py:12
  26.7 3.2 %collective-permute-start.2 = (bf16[128,1152]{1,0:T(8,128)(2,1)S(1)}, bf16[128,1152]{1,0:T(8,128)(2,1)S(1)}, u32[]{:S(2)}, u32[]{:S(2)}) collective-permute-start(bf16[128,1152]{1,0:T(8,128)(2,1)S(1)} %collective-permute-done.1), channel_id=1, source_target_pairs={{0,4},{4,8},{8,12},{12,16},{16,20},{20,24},{24,28},{28,32},{32,36}... | collective-permute-start | bytes 884744 | tf_op jit(solution)/shard_map/ppermute | solution.py:12
  29.9 0.3 fusion.20
  30.2 0.2 convolution_add_fusion
  30.4 6.1 %collective-permute-start.9 = (f32[128,1152]{1,0:T(8,128)S(1)}, f32[128,1152]{1,0:T(8,128)S(1)}, u32[]{:S(2)}, u32[]{:S(2)}) collective-permute-start(f32[128,1152]{1,0:T(8,128)S(1)} %convolution_add_fusion), channel_id=1, source_target_pairs={{0,4},{4,8},{8,12},{12,16},{16,20},{20,24},{24,28},{28,32},{32,36}... | collective-permute-start | bytes 1769480 | tf_op jit(solution)/shard_map/ppermute | solution.py:12
  36.6 0.3 fusion.29
  36.8 2.8 %collective-permute-start.3 = (bf16[128,1152]{1,0:T(8,128)(2,1)S(1)}, bf16[128,1152]{1,0:T(8,128)(2,1)S(1)}, u32[]{:S(2)}, u32[]{:S(2)}) collective-permute-start(bf16[128,1152]{1,0:T(8,128)(2,1)S(1)} %collective-permute-done.2), channel_id=1, source_target_pairs={{0,4},{4,8},{8,12},{12,16},{16,20},{20,24},{24,28},{28,32},{32,36}... | collective-permute-start | bytes 884744 | tf_op jit(solution)/shard_map/ppermute | solution.py:12
  39.6 0.3 fusion.21
  40.2 1.4 collective-permute-done.9
  41.7 4.3 %collective-permute-start.10 = (f32[128,1152]{1,0:T(8,128)S(1)}, f32[128,1152]{1,0:T(8,128)S(1)}, u32[]{:S(2)}, u32[]{:S(2)}) collective-permute-start(f32[128,1152]{1,0:T(8,128)S(1)} %add.211), channel_id=1, source_target_pairs={{0,4},{4,8},{8,12},{12,16},{16,20},{20,24},{24,28},{28,32},{32,36}... | collective-permute-start | bytes 1769480 | tf_op jit(solution)/shard_map/ppermute | solution.py:12
  46.0 0.3 fusion.1
  46.3 5.6 %collective-permute-start.4 = (bf16[128,1152]{1,0:T(8,128)(2,1)S(1)}, bf16[128,1152]{1,0:T(8,128)(2,1)S(1)}, u32[]{:S(2)}, u32[]{:S(2)}) collective-permute-start(bf16[128,1152]{1,0:T(8,128)(2,1)S(1)} %collective-permute-done.3), channel_id=1, source_target_pairs={{0,4},{4,8},{8,12},{12,16},{16,20},{20,24},{24,28},{28,32},{32,36}... | collective-permute-start | bytes 884744 | tf_op jit(solution)/shard_map/ppermute | solution.py:12
  51.9 0.3 fusion.22
  52.5 0.4 collective-permute-done.10
  53.0 5.6 %collective-permute-start.11 = (f32[128,1152]{1,0:T(8,128)S(1)}, f32[128,1152]{1,0:T(8,128)S(1)}, u32[]{:S(2)}, u32[]{:S(2)}) collective-permute-start(f32[128,1152]{1,0:T(8,128)S(1)} %add.212), channel_id=1, source_target_pairs={{0,4},{4,8},{8,12},{12,16},{16,20},{20,24},{24,28},{28,32},{32,36}... | collective-permute-start | bytes 1769480 | tf_op jit(solution)/shard_map/ppermute | solution.py:12
  58.5 0.3 convolution_add_fusion.6
  58.8 5.6 %collective-permute-start.5 = (bf16[128,1152]{1,0:T(8,128)(2,1)S(1)}, bf16[128,1152]{1,0:T(8,128)(2,1)S(1)}, u32[]{:S(2)}, u32[]{:S(2)}) collective-permute-start(bf16[128,1152]{1,0:T(8,128)(2,1)S(1)} %collective-permute-done.4), channel_id=1, source_target_pairs={{0,4},{4,8},{8,12},{12,16},{16,20},{20,24},{24,28},{28,32},{32,36}... | collective-permute-start | bytes 884744 | tf_op jit(solution)/shard_map/ppermute | solution.py:12
  64.4 0.3 fusion.23
  64.7 0.2 fusion.32
  65.0 5.9 %collective-permute-start.12 = (f32[128,1152]{1,0:T(8,128)S(1)}, f32[128,1152]{1,0:T(8,128)S(1)}, u32[]{:S(2)}, u32[]{:S(2)}) collective-permute-start(f32[128,1152]{1,0:T(8,128)S(1)} %add.213), channel_id=1, source_target_pairs={{0,4},{4,8},{8,12},{12,16},{16,20},{20,24},{24,28},{28,32},{32,36}... | collective-permute-start | bytes 1769480 | tf_op jit(solution)/shard_map/ppermute | solution.py:12
  71.0 0.3 convolution_add_fusion.5
  71.3 5.6 %collective-permute-start.6 = (bf16[128,1152]{1,0:T(8,128)(2,1)S(1)}, bf16[128,1152]{1,0:T(8,128)(2,1)S(1)}, u32[]{:S(2)}, u32[]{:S(2)}) collective-permute-start(bf16[128,1152]{1,0:T(8,128)(2,1)S(1)} %collective-permute-done.5), channel_id=1, source_target_pairs={{0,4},{4,8},{8,12},{12,16},{16,20},{20,24},{24,28},{28,32},{32,36}... | collective-permute-start | bytes 884744 | tf_op jit(solution)/shard_map/ppermute | solution.py:12
  76.9 0.3 fusion.24
  77.5 6.0 %collective-permute-start.13 = (f32[128,1152]{1,0:T(8,128)S(1)}, f32[128,1152]{1,0:T(8,128)S(1)}, u32[]{:S(2)}, u32[]{:S(2)}) collective-permute-start(f32[128,1152]{1,0:T(8,128)S(1)} %add.214), channel_id=1, source_target_pairs={{0,4},{4,8},{8,12},{12,16},{16,20},{20,24},{24,28},{28,32},{32,36}... | collective-permute-start | bytes 1769480 | tf_op jit(solution)/shard_map/ppermute | solution.py:12
  83.5 0.3 convolution_add_fusion.4
  83.8 5.6 %collective-permute-start.7 = (bf16[128,1152]{1,0:T(8,128)(2,1)S(1)}, bf16[128,1152]{1,0:T(8,128)(2,1)S(1)}, u32[]{:S(2)}, u32[]{:S(2)}) collective-permute-start(bf16[128,1152]{1,0:T(8,128)(2,1)S(1)} %collective-permute-done.6), channel_id=1, source_target_pairs={{0,4},{4,8},{8,12},{12,16},{16,20},{20,24},{24,28},{28,32},{32,36}... | collective-permute-start | bytes 884744 | tf_op jit(solution)/shard_map/ppermute | solution.py:12
  89.4 0.3 fusion.25
  89.7 0.2 fusion.34
  90.0 6.0 %collective-permute-start.14 = (f32[128,1152]{1,0:T(8,128)S(1)}, f32[128,1152]{1,0:T(8,128)S(1)}, u32[]{:S(2)}, u32[]{:S(2)}) collective-permute-start(f32[128,1152]{1,0:T(8,128)S(1)} %add.215), channel_id=1, source_target_pairs={{0,4},{4,8},{8,12},{12,16},{16,20},{20,24},{24,28},{28,32},{32,36}... | collective-permute-start | bytes 1769480 | tf_op jit(solution)/shard_map/ppermute | solution.py:12
  95.9 0.3 convolution_add_fusion.3
  96.2 0.3 fusion.26
  96.5 0.2 fusion.35
  96.8 4.4 %collective-permute-done.14 = f32[128,1152]{1,0:T(8,128)S(1)} collective-permute-done((f32[128,1152]{1,0:T(8,128)S(1)}, f32[128,1152]{1,0:T(8,128)S(1)}, u32[]{:S(2)}, u32[]{:S(2)}) %collective-permute-start.14) | collective-permute-done | bytes 589856 | tf_op jit(solution)/shard_map/ppermute | solution.py:12
  101.3 18.0 %collective-permute-start.15 = (f32[128,1152]{1,0:T(8,128)S(1)}, f32[128,1152]{1,0:T(8,128)S(1)}, u32[]{:S(2)}, u32[]{:S(2)}) collective-permute-start(f32[128,1152]{1,0:T(8,128)S(1)} %add.216), channel_id=1, source_target_pairs={{0,996},{4,1000},{8,1004},{12,1008},{16,1012},{20,1016},{24,1020},... | collective-permute-start | bytes 1769480 | tf_op jit(solution)/shard_map/ppermute | solution.py:12
  119.3 0.3 convolution_add_fusion.2
  119.6 0.5 add_add_fusion
  120.1 1.1 fusion
  121.2 37.5 %collective-permute-done.15 = f32[128,1152]{1,0:T(8,128)S(1)} collective-permute-done((f32[128,1152]{1,0:T(8,128)S(1)}, f32[128,1152]{1,0:T(8,128)S(1)}, u32[]{:S(2)}, u32[]{:S(2)}) %collective-permute-start.15) | collective-permute-done | bytes 589856 | tf_op jit(solution)/shard_map/ppermute | solution.py:12
  158.7 0.9 add_multiply_fusion
  (25 shorter events, 1.1 us)
Async XLA Ops:
  0.6 8.1 %copy-start = (bf16[128,1152]{1,0:T(8,128)(2,1)S(1)}, bf16[128,1152]{1,0:T(8,128)(2,1)}, u32[]{:S(2)}) copy-start(bf16[128,1152]{1,0:T(8,128)(2,1)} %param.4) | copy-start | bytes 884740
  0.6 26.0 %collective-permute-start.1 = (bf16[128,1152]{1,0:T(8,128)(2,1)}, bf16[128,1152]{1,0:T(8,128)(2,1)S(1)}, u32[]{:S(2)}, u32[]{:S(2)}) collective-permute-start(bf16[128,1152]{1,0:T(8,128)(2,1)} %param.5), channel_id=1, source_target_pairs={{0,4},{4,8},{8,12},{12,16},{16,20},{20,24},{24,28},{28,32},{32,36}... | collective-permute-start | bytes 884744 | tf_op jit(solution)/shard_map/ppermute | solution.py:12
  2.7 18.9 %collective-permute-start = (bf16[128,1152]{1,0:T(8,128)(2,1)}, bf16[128,1152]{1,0:T(8,128)(2,1)S(1)}, u32[]{:S(2)}, u32[]{:S(2)}) collective-permute-start(bf16[128,1152]{1,0:T(8,128)(2,1)} %param.5), channel_id=1, source_target_pairs={{0,1},{1,2},{2,3},{3,0},{4,5},{5,6},{6,7},{7,4},{8,9},{9,10},{10,1... | collective-permute-start | bytes 884744 | tf_op jit(solution)/shard_map/ppermute | solution.py:12
  10.0 6.5 %copy-start.1 = (bf16[128,1152]{1,0:T(8,128)(2,1)S(1)}, bf16[128,1152]{1,0:T(8,128)(2,1)}, u32[]{:S(2)}) copy-start(bf16[128,1152]{1,0:T(8,128)(2,1)} %param.5) | copy-start | bytes 884740
  10.3 19.9 %collective-permute-start.8 = (f32[128,1152]{1,0:T(8,128)S(1)}, f32[128,1152]{1,0:T(8,128)S(1)}, u32[]{:S(2)}, u32[]{:S(2)}) collective-permute-start(f32[128,1152]{1,0:T(8,128)S(1)} %fusion.36), channel_id=1, source_target_pairs={{0,4},{4,8},{8,12},{12,16},{16,20},{20,24},{24,28},{28,32},{32,36}... | collective-permute-start | bytes 1769480 | tf_op jit(solution)/shard_map/ppermute | solution.py:12
  22.2 99.0 %collective-permute-start.16 = (f32[128,1152]{1,0:T(8,128)S(1)}, f32[128,1152]{1,0:T(8,128)S(1)}, u32[]{:S(2)}, u32[]{:S(2)}) collective-permute-start(f32[128,1152]{1,0:T(8,128)S(1)} %fusion.28), channel_id=1, source_target_pairs={{0,3},{1,0},{2,1},{3,2},{4,7},{5,4},{6,5},{7,6},{8,11},{9,8},{10,9... | collective-permute-start | bytes 1769480 | tf_op jit(solution)/shard_map/ppermute | solution.py:12
  26.7 10.2 %collective-permute-start.2 = (bf16[128,1152]{1,0:T(8,128)(2,1)S(1)}, bf16[128,1152]{1,0:T(8,128)(2,1)S(1)}, u32[]{:S(2)}, u32[]{:S(2)}) collective-permute-start(bf16[128,1152]{1,0:T(8,128)(2,1)S(1)} %collective-permute-done.1), channel_id=1, source_target_pairs={{0,4},{4,8},{8,12},{12,16},{16,20},{20,24},{24,28},{28,32},{32,36}... | collective-permute-start | bytes 884744 | tf_op jit(solution)/shard_map/ppermute | solution.py:12
  30.4 11.2 %collective-permute-start.9 = (f32[128,1152]{1,0:T(8,128)S(1)}, f32[128,1152]{1,0:T(8,128)S(1)}, u32[]{:S(2)}, u32[]{:S(2)}) collective-permute-start(f32[128,1152]{1,0:T(8,128)S(1)} %convolution_add_fusion), channel_id=1, source_target_pairs={{0,4},{4,8},{8,12},{12,16},{16,20},{20,24},{24,28},{28,32},{32,36}... | collective-permute-start | bytes 1769480 | tf_op jit(solution)/shard_map/ppermute | solution.py:12
  36.8 9.5 %collective-permute-start.3 = (bf16[128,1152]{1,0:T(8,128)(2,1)S(1)}, bf16[128,1152]{1,0:T(8,128)(2,1)S(1)}, u32[]{:S(2)}, u32[]{:S(2)}) collective-permute-start(bf16[128,1152]{1,0:T(8,128)(2,1)S(1)} %collective-permute-done.2), channel_id=1, source_target_pairs={{0,4},{4,8},{8,12},{12,16},{16,20},{20,24},{24,28},{28,32},{32,36}... | collective-permute-start | bytes 884744 | tf_op jit(solution)/shard_map/ppermute | solution.py:12
  41.7 11.2 %collective-permute-start.10 = (f32[128,1152]{1,0:T(8,128)S(1)}, f32[128,1152]{1,0:T(8,128)S(1)}, u32[]{:S(2)}, u32[]{:S(2)}) collective-permute-start(f32[128,1152]{1,0:T(8,128)S(1)} %add.211), channel_id=1, source_target_pairs={{0,4},{4,8},{8,12},{12,16},{16,20},{20,24},{24,28},{28,32},{32,36}... | collective-permute-start | bytes 1769480 | tf_op jit(solution)/shard_map/ppermute | solution.py:12
  46.3 12.5 %collective-permute-start.4 = (bf16[128,1152]{1,0:T(8,128)(2,1)S(1)}, bf16[128,1152]{1,0:T(8,128)(2,1)S(1)}, u32[]{:S(2)}, u32[]{:S(2)}) collective-permute-start(bf16[128,1152]{1,0:T(8,128)(2,1)S(1)} %collective-permute-done.3), channel_id=1, source_target_pairs={{0,4},{4,8},{8,12},{12,16},{16,20},{20,24},{24,28},{28,32},{32,36}... | collective-permute-start | bytes 884744 | tf_op jit(solution)/shard_map/ppermute | solution.py:12
  53.0 12.0 %collective-permute-start.11 = (f32[128,1152]{1,0:T(8,128)S(1)}, f32[128,1152]{1,0:T(8,128)S(1)}, u32[]{:S(2)}, u32[]{:S(2)}) collective-permute-start(f32[128,1152]{1,0:T(8,128)S(1)} %add.212), channel_id=1, source_target_pairs={{0,4},{4,8},{8,12},{12,16},{16,20},{20,24},{24,28},{28,32},{32,36}... | collective-permute-start | bytes 1769480 | tf_op jit(solution)/shard_map/ppermute | solution.py:12
  58.8 12.5 %collective-permute-start.5 = (bf16[128,1152]{1,0:T(8,128)(2,1)S(1)}, bf16[128,1152]{1,0:T(8,128)(2,1)S(1)}, u32[]{:S(2)}, u32[]{:S(2)}) collective-permute-start(bf16[128,1152]{1,0:T(8,128)(2,1)S(1)} %collective-permute-done.4), channel_id=1, source_target_pairs={{0,4},{4,8},{8,12},{12,16},{16,20},{20,24},{24,28},{28,32},{32,36}... | collective-permute-start | bytes 884744 | tf_op jit(solution)/shard_map/ppermute | solution.py:12
  65.0 12.4 %collective-permute-start.12 = (f32[128,1152]{1,0:T(8,128)S(1)}, f32[128,1152]{1,0:T(8,128)S(1)}, u32[]{:S(2)}, u32[]{:S(2)}) collective-permute-start(f32[128,1152]{1,0:T(8,128)S(1)} %add.213), channel_id=1, source_target_pairs={{0,4},{4,8},{8,12},{12,16},{16,20},{20,24},{24,28},{28,32},{32,36}... | collective-permute-start | bytes 1769480 | tf_op jit(solution)/shard_map/ppermute | solution.py:12
  71.3 12.5 %collective-permute-start.6 = (bf16[128,1152]{1,0:T(8,128)(2,1)S(1)}, bf16[128,1152]{1,0:T(8,128)(2,1)S(1)}, u32[]{:S(2)}, u32[]{:S(2)}) collective-permute-start(bf16[128,1152]{1,0:T(8,128)(2,1)S(1)} %collective-permute-done.5), channel_id=1, source_target_pairs={{0,4},{4,8},{8,12},{12,16},{16,20},{20,24},{24,28},{28,32},{32,36}... | collective-permute-start | bytes 884744 | tf_op jit(solution)/shard_map/ppermute | solution.py:12
  77.5 12.4 %collective-permute-start.13 = (f32[128,1152]{1,0:T(8,128)S(1)}, f32[128,1152]{1,0:T(8,128)S(1)}, u32[]{:S(2)}, u32[]{:S(2)}) collective-permute-start(f32[128,1152]{1,0:T(8,128)S(1)} %add.214), channel_id=1, source_target_pairs={{0,4},{4,8},{8,12},{12,16},{16,20},{20,24},{24,28},{28,32},{32,36}... | collective-permute-start | bytes 1769480 | tf_op jit(solution)/shard_map/ppermute | solution.py:12
  83.8 12.5 %collective-permute-start.7 = (bf16[128,1152]{1,0:T(8,128)(2,1)S(1)}, bf16[128,1152]{1,0:T(8,128)(2,1)S(1)}, u32[]{:S(2)}, u32[]{:S(2)}) collective-permute-start(bf16[128,1152]{1,0:T(8,128)(2,1)S(1)} %collective-permute-done.6), channel_id=1, source_target_pairs={{0,4},{4,8},{8,12},{12,16},{16,20},{20,24},{24,28},{28,32},{32,36}... | collective-permute-start | bytes 884744 | tf_op jit(solution)/shard_map/ppermute | solution.py:12
  90.0 11.2 %collective-permute-start.14 = (f32[128,1152]{1,0:T(8,128)S(1)}, f32[128,1152]{1,0:T(8,128)S(1)}, u32[]{:S(2)}, u32[]{:S(2)}) collective-permute-start(f32[128,1152]{1,0:T(8,128)S(1)} %add.215), channel_id=1, source_target_pairs={{0,4},{4,8},{8,12},{12,16},{16,20},{20,24},{24,28},{28,32},{32,36}... | collective-permute-start | bytes 1769480 | tf_op jit(solution)/shard_map/ppermute | solution.py:12
  101.3 57.5 %collective-permute-start.15 = (f32[128,1152]{1,0:T(8,128)S(1)}, f32[128,1152]{1,0:T(8,128)S(1)}, u32[]{:S(2)}, u32[]{:S(2)}) collective-permute-start(f32[128,1152]{1,0:T(8,128)S(1)} %add.216), channel_id=1, source_target_pairs={{0,996},{4,1000},{8,1004},{12,1008},{16,1012},{20,1016},{24,1020},... | collective-permute-start | bytes 1769480 | tf_op jit(solution)/shard_map/ppermute | solution.py:12
where the time goes:
time: 160 us
  starting transfers between devices  97.8 us (61%)
  waiting for transfers between devices  48.7 us (30%)
  matrix products  9.01 us (6%)
  between operations  2.33 us (1%)
  other arithmetic  1.77 us (1%)
    ppermute x17, starting transfers between devices, shifted(): return lax.ppermute(value, axis, pairs)  97.8 us
    ppermute x17, waiting for transfers between devices, shifted(): return lax.ppermute(value, axis, pairs)  48.7 us
    dot_general x9, matrix products, tile_coef(): lax.dot_general(images, partner, (((1,), (1,)), ((), ())), preferred_elem...  3.7 us
    dot_general x9, matrix products, pair_block(): grad_img = jnp.dot(coef, partner, preferred_element_type=jnp.float32)  3.28 us
  transfers between devices with their start and end apart: 17, of which 5 were waited for; matrix products, arithmetic and copies ran while one was open for 6% of the time, Pallas kernels for 0%

commit v1 on v0

v1 whole, which is shorter than its diff:
```python
import functools

import jax
import jax.numpy as jnp
from jax import lax
from jax.experimental import pallas as pl
from jax.experimental.pallas import tpu as pltpu
from jax.sharding import PartitionSpec as P

HOPS = 3
CHUNKS = 2
VMEM_LIMIT = 48 * 2**20
MESH = pl.DeviceIdType.MESH


def kernel(
    n_blk,
    n_grp,
    images,
    texts,
    scale_in,
    bias_in,
    loss_out,
    grad_out,
    own,
    pair,
    ext,
    cross,
    acc,
    lacc,
    load_sem,
    send_sem,
    hop_send,
    hop_sem,
    sib_sem,
    ext_sem,
    cross_sem,
    ready_sem,
    scale,
    bias,
):
    rows = own.shape[1]
    piece = rows // CHUNKS
    b = lax.axis_index("blk")
    g = lax.axis_index("grp")
    c = lax.rem(b, 2)
    z = lax.rem(b // 2, 8)

    def at(db, dg=0):
        return (lax.rem(b + db + n_blk, n_blk), lax.rem(g + dg + n_grp, n_grp))

    sib = at(1 - 2 * c)
    along = (at(2), at(-2))
    along2 = (at(4), at(-4))
    nextdoor = (at(1), at(-1))
    over = (at(0, 1), at(0, -1))
    source = (texts, images)

    loads = [
        pltpu.make_async_copy(images, own.at[0], load_sem.at[0]),
        pltpu.make_async_copy(texts, own.at[1], load_sem.at[1]),
        pltpu.make_async_copy(scale_in, scale, load_sem.at[2]),
        pltpu.make_async_copy(bias_in, bias, load_sem.at[3]),
    ]
    for load in loads:
        load.start()

    first, last = z == 0, z == 7
    inner_up, inner_down = z != 7, z != 0
    greets = (
        (along[0], inner_up),
        (along[1], first),
        (nextdoor[0], jnp.logical_or(c == 0, inner_up)),
        (nextdoor[1], jnp.logical_and(c == 0, first)),
        (over[0], g < 2),
        (over[1], jnp.logical_or(g == 0, g == 3)),
    )
    greeted = (
        (along[0], last),
        (along[1], inner_down),
        (nextdoor[0], jnp.logical_and(c == 1, last)),
        (nextdoor[1], jnp.logical_or(c == 1, inner_down)),
        (over[0], jnp.logical_or(g == 2, g == 3)),
        (over[1], jnp.logical_or(g == 1, g == 2)),
    )
    mirror = (1, 0, 3, 2, 5, 4)
    barrier = pltpu.get_barrier_semaphore()
    for device, when in greets:

        @pl.when(when)
        def _():
            pl.semaphore_signal(barrier, inc=1, device_id=device, device_id_type=MESH)

    here_first = sum(jnp.where(when, 1, 0) for _, when in greeted)

    @pl.when(here_first > 0)
    def _():
        pl.semaphore_wait(barrier, here_first)

    for n, (device, when) in enumerate(greeted):

        @pl.when(when)
        def _():
            pl.semaphore_signal(
                ready_sem.at[mirror[n]], inc=1, device_id=device, device_id_type=MESH
            )

    def ready(n, when):
        @pl.when(jnp.logical_and(greets[n][1], when))
        def _():
            pl.semaphore_wait(ready_sem.at[n], 1)

    sent = []

    def copy_to(src, dst, recv, device, sem):
        return pltpu.make_async_remote_copy(
            src_ref=src,
            dst_ref=dst,
            send_sem=sem,
            recv_sem=recv,
            device_id=device,
            device_id_type=MESH,
        )

    def send(src, dst, recv, device, when):
        copy = copy_to(src, dst, recv, device, send_sem.at[len(sent)])
        sent.append((copy, when))
        pl.when(when)(copy.start)

    def arrived(dst, recv):
        pltpu.make_async_remote_copy(
            src_ref=dst,
            dst_ref=dst,
            send_sem=send_sem.at[0],
            recv_sem=recv,
            device_id=sib,
            device_id_type=MESH,
        ).wait_recv()

    def part(k):
        return pl.ds(k * piece, piece)

    def lane(s, hop, k, core):
        start = pl.multiple_of(core * rows + k * piece, piece)
        return pair.at[s, hop, pl.ds(start, piece), :]

    def send_own(s, when):
        for k in range(CHUNKS):
            send(source[s].at[part(k)], lane(s, 0, k, c), hop_sem.at[s, 0, k], along[s], when)

    def send_cross(when):
        for s in range(2):
            send(source[s], cross.at[s], cross_sem.at[s], over[s], when)

    send_own(1, inner_down)
    send(images, ext.at[1], ext_sem.at[1], nextdoor[1], c == 1)
    ready(0, inner_up)
    send_own(0, g >= 0)
    ready(2, c == 0)
    send(texts, ext.at[0], ext_sem.at[0], nextdoor[0], c == 0)
    ready(4, g >= 0)
    ready(5, g >= 0)
    send_cross(inner_up)

    def meet(side, block, positive=False, first=False):
        values = block[...]
        dots = lax.dot_general(
            own[side], values, (((1,), (1,)), ((), ())), preferred_element_type=jnp.float32
        )
        score = factor * dots + offset
        if positive:
            diagonal = lax.broadcasted_iota(jnp.int32, score.shape, 0) == lax.broadcasted_iota(
                jnp.int32, score.shape, 1
            )
            score = jnp.where(diagonal, -score, score)
        small = jnp.exp(-jnp.abs(score))
        share = 1.0 / (1.0 + small)
        coef = jnp.where(score >= 0, share, small * share)
        if positive:
            coef = jnp.where(diagonal, -coef, coef)
        term = jnp.maximum(score, 0.0) + jnp.log1p(small)
        if score.shape[1] > rows:
            term = term[:, :rows] + term[:, rows:]
        grad = jnp.dot(coef.astype(jnp.bfloat16), values, preferred_element_type=jnp.float32)
        if first:
            lacc[side] = term
            acc[side] = grad
        else:
            lacc[side] += term
            acc[side] += grad

    for load in loads:
        load.wait()
    factor, offset = scale[0], bias[0]
    for side in range(2):
        meet(side, own.at[1 - side], positive=True, first=True)

    def meet_cross(when):
        @pl.when(when)
        def _():
            for s in range(2):
                arrived(cross.at[s], cross_sem.at[s])

            @pl.loop(0, 2)
            def _(s):
                meet(s, cross.at[s])

    ready(2, c == 1)
    meet_cross(first)
    ready(1, first)
    ready(3, first)
    send_own(1, first)

    code = jnp.where(first, 19, jnp.where(z == 1, 22, jnp.where(last, 50, 42)))

    def stream_hop(i):
        s = lax.rem(code // (1 << i), 2)
        ups = sum(lax.rem(code // (1 << j), 2) for j in range(i)) if i else 0
        return s, jnp.where(s == 1, ups, i - ups)

    steps = [stream_hop(i) for i in range(2 * HOPS)]

    def forwards(i, k):
        s, hop = steps[i]
        here = lane(s, hop, k, c)
        further = lane(s, lax.rem(hop + 1, HOPS), k, c)
        n = i * CHUNKS + k
        return (
            (
                copy_to(here, further, hop_sem.at[s, lax.rem(hop + 1, HOPS), k], at(2 - 4 * s), hop_send.at[n, 0]),
                hop + 1 < HOPS,
            ),
            (
                copy_to(here, ext.at[s, part(k)], late_sem(ext_sem, s, k), at(1 - 2 * s), hop_send.at[n, 0]),
                jnp.logical_and(hop + 1 == HOPS, c == 1 - s),
            ),
            (copy_to(here, here, sib_sem.at[s, hop, k], sib, hop_send.at[n, 1]), g >= 0),
        )

    for i in range(2 * HOPS + 1):
        if i < 2 * HOPS:
            s, hop = steps[i]
            for k in range(CHUNKS):
                arrived(lane(s, hop, k, c), hop_sem.at[s, hop, k])
                for copy, when in forwards(i, k):
                    pl.when(when)(copy.start)
        if i == 1:
            early = 1 - c
            arrived(ext.at[early], ext_sem.at[early])
            meet(early, ext.at[early])
        if i == 3:
            meet_cross(jnp.logical_and(inner_up, inner_down))
            send_cross(last)
        if i >= 1:
            s, hop = steps[i - 1]
            for k in range(CHUNKS):
                arrived(lane(s, hop, k, 1 - c), sib_sem.at[s, hop, k])
            meet(s, pair.at[s, hop])
    meet_cross(last)
    for k in range(CHUNKS):
        arrived(ext.at[c, part(k)], late_sem(ext_sem, c, k))
    meet(c, ext.at[c])

    for side in range(2):
        grad_out[side] = factor * acc[side]
    loss_out[...] = jnp.sum(lacc[0].T, axis=0, keepdims=True)
    for copy, when in sent:
        pl.when(when)(copy.wait_send)
    for i in range(2 * HOPS):
        for k in range(CHUNKS):
            for copy, when in forwards(i, k):
                pl.when(when)(copy.wait_send)


def late_sem(ext_sem, s, k):
    return ext_sem.at[2 + 2 * k + s]


def hand_over(loss_in, grad_in, loss_out, gimg_out, gtxt_out, sem):
    half = gimg_out.shape[0] // 2
    copies = [pltpu.make_async_copy(loss_in, loss_out, sem.at[4])]
    for side, out in enumerate((gimg_out, gtxt_out)):
        for k in range(2):
            rows = pl.ds(k * half, half)
            copies.append(
                pltpu.make_async_copy(grad_in.at[side, rows], out.at[rows], sem.at[2 * side + k])
            )
    for copy in copies:
        copy.start()
    for copy in copies:
        copy.wait()


def solution(mesh):
    n_blk, n_grp = mesh.shape["blk"], mesh.shape["grp"]

    def on_device(images, texts, scale, bias):
        rows, width = images.shape
        bf16, f32 = jnp.bfloat16, jnp.float32
        hbm = pl.BlockSpec(memory_space=pltpu.HBM)
        vmem = pl.BlockSpec(memory_space=pltpu.VMEM)
        anywhere = pl.BlockSpec(memory_space=pl.ANY)
        loss, grads = pl.pallas_call(
            functools.partial(kernel, n_blk, n_grp),
            out_shape=(
                jax.ShapeDtypeStruct((1, rows), f32),
                jax.ShapeDtypeStruct((2, rows, width), f32),
            ),
            in_specs=[hbm] * 4,
            out_specs=(vmem, vmem),
            scratch_shapes=[
                pltpu.VMEM((2, rows, width), bf16),
                pltpu.VMEM((2, HOPS, 2 * rows, width), bf16),
                pltpu.VMEM((2, rows, width), bf16),
                pltpu.VMEM((2, rows, width), bf16),
                pltpu.VMEM((2, rows, width), f32),
                pltpu.VMEM((2, rows, rows), f32),
                pltpu.SemaphoreType.DMA((4,)),
                pltpu.SemaphoreType.DMA((3 * CHUNKS + 6,)),
                pltpu.SemaphoreType.DMA((2 * HOPS * CHUNKS, 2)),
                pltpu.SemaphoreType.DMA((2, HOPS, CHUNKS)),
                pltpu.SemaphoreType.DMA((2, HOPS, CHUNKS)),
                pltpu.SemaphoreType.DMA((2 + 2 * CHUNKS,)),
                pltpu.SemaphoreType.DMA((2,)),
                pltpu.SemaphoreType.REGULAR((6,)),
                pltpu.SMEM((1,), f32),
                pltpu.SMEM((1,), f32),
            ],
            compiler_params=pltpu.CompilerParams(
                collective_id=0, has_side_effects=True, vmem_limit_bytes=VMEM_LIMIT
            ),
        )(images, texts, scale, bias)
        loss, gimg, gtxt = pl.pallas_call(
            hand_over,
            out_shape=(
                jax.ShapeDtypeStruct((1, rows), f32),
                jax.ShapeDtypeStruct((rows, width), f32),
                jax.ShapeDtypeStruct((rows, width), f32),
            ),
            in_specs=[anywhere] * 2,
            out_specs=(anywhere,) * 3,
            scratch_shapes=[pltpu.SemaphoreType.DMA((5,))],
            compiler_params=pltpu.CompilerParams(vmem_limit_bytes=VMEM_LIMIT),
        )(loss, grads)
        return loss.reshape(rows), gimg, gtxt

    block = P(("blk", "grp"), None)
    return jax.shard_map(
        on_device,
        mesh=mesh,
        in_specs=(block, block, P(), P()),
        out_specs=(P(("blk", "grp")), block, block),
        check_vma=False,
    )
```

time: 160 us -> 61.4 us (0.38)
  the two profiles are of different devices: /device:TPU:414 before, /device:TPU:1 now
where the time goes in v1:
time: 61.4 us; the launch traced here: 61 us
  Pallas kernels  57.1 us (93%)
  between operations  1.94 us (3%)
  local copies, waits for them, and re-layouts  1.92 us (3%)
    pallas_call x1, Pallas kernels, on_device(): pl.pallas_call(functools.partial(kernel, n_blk, n_grp), out_shape=(jax.Sh...  56.1 us
    unnamed x4, local copies, waits for them, and re-layouts  1.92 us

profile of v1, /device:TPU:1, one launch (start us, length us, event | category | flops | bytes accessed | tf_op | source)
XLA Modules:
  0.0 61.0 jit_solution(12971609216595607932)
XLA Ops:
  1.9 0.0 copy-start
  1.9 1.0 %copy-done = bf16[128,1152]{1,0:T(8,128)(2,1)S(1)} copy-done((bf16[128,1152]{1,0:T(8,128)(2,1)S(1)}, bf16[128,1152]{1,0:T(8,128)(2,1)}, u32[]{:S(2)}) %copy-start) | copy-done | bytes 294936
  2.9 0.0 copy-start.1
  2.9 1.0 %copy-done.1 = bf16[128,1152]{1,0:T(8,128)(2,1)S(1)} copy-done((bf16[128,1152]{1,0:T(8,128)(2,1)S(1)}, bf16[128,1152]{1,0:T(8,128)(2,1)}, u32[]{:S(2)}) %copy-start.1) | copy-done | bytes 294936
  3.8 56.1 %shard_map.67 = (f32[1,128]{1,0:T(1,128)S(1)}, f32[2,128,1152]{2,1,0:T(8,128)S(1)}) custom-call(bf16[128,1152]{1,0:T(8,128)(2,1)S(1)} %copy-done, bf16[128,1152]{1,0:T(8,128)(2,1)S(1)} %copy-done.1, f32[1]{0:T(128)S(6)} %copy.7.scale_in, f32[1]{0:T(128)S(6)} %copy.8.bias_in), custom_call_target="tpu_custom_call" | custom-call | tf_op jit(solution)/shard_map/pallas_call | solution.py:303
  59.9 1.1 %shard_map.68 = (f32[1,128]{1,0:T(1,128)}, f32[128,1152]{1,0:T(8,128)}, f32[128,1152]{1,0:T(8,128)}) custom-call(f32[1,128]{1,0:T(1,128)S(1)} %get-tuple-element.8.loss_in, f32[2,128,1152]{2,1,0:T(8,128)S(1)} %get-tuple-element.9.grad_in), custom_call_target="tpu_custom_call" | custom-call | tf_op jit(solution)/shard_map/pallas_call | solution.py:333
Async XLA Ops:
  1.9 1.0 %copy-start = (bf16[128,1152]{1,0:T(8,128)(2,1)S(1)}, bf16[128,1152]{1,0:T(8,128)(2,1)}, u32[]{:S(2)}) copy-start(bf16[128,1152]{1,0:T(8,128)(2,1)} %images.1) | copy-start | bytes 884740
  2.9 1.0 %copy-start.1 = (bf16[128,1152]{1,0:T(8,128)(2,1)S(1)}, bf16[128,1152]{1,0:T(8,128)(2,1)}, u32[]{:S(2)}) copy-start(bf16[128,1152]{1,0:T(8,128)(2,1)} %texts.1) | copy-start | bytes 884740

commit v2 on v1

--- a/solution.py
+++ b/solution.py
@@ -8,7 +8,9 @@
 from jax.sharding import PartitionSpec as P
 
 HOPS = 3
-CHUNKS = 2
+CHUNKS = 4
+RELAY_AT = 2
+CROSS_AT = 0
 VMEM_LIMIT = 48 * 2**20
 MESH = pl.DeviceIdType.MESH
 
@@ -29,6 +31,8 @@
     acc,
     lacc,
     load_sem,
+    relay,
+    relay_sem,
     send_sem,
     hop_send,
     hop_sem,
@@ -46,6 +50,9 @@
     c = lax.rem(b, 2)
     z = lax.rem(b // 2, 8)
 
+    def is_root(device):
+        return jnp.logical_and(device[0] == 0, device[1] == 0)
+
     def at(db, dg=0):
         return (lax.rem(b + db + n_blk, n_blk), lax.rem(g + dg + n_grp, n_grp))
 
@@ -84,14 +91,41 @@
         (over[1], jnp.logical_or(g == 1, g == 2)),
     )
     mirror = (1, 0, 3, 2, 5, 4)
+    root = is_root((b, g))
+    def flips(n, to):
+        near_root = jnp.logical_and(is_root(to), z != 7)
+        return near_root if n in (1, 3) else jnp.logical_or(root, near_root)
+
+    greets = tuple(
+        (to, jnp.where(flips(n, to), ~root, when)) for n, (to, when) in enumerate(greets)
+    )
+    greeted = tuple(
+        (to, jnp.where(flips(n, to), root, when)) for n, (to, when) in enumerate(greeted)
+    )
+    far_to_root = jnp.logical_and(z == 3, jnp.where(c == 0, is_root(at(10)), is_root(at(9))))
+    even, odd = c == 0, c == 1
+    far_greets = (
+        (at(-4), first),
+        (at(-6), jnp.logical_and(first, odd)),
+        (at(-9), jnp.logical_and(first, jnp.logical_and(even, ~root))),
+        (at(-10), jnp.logical_and(first, jnp.logical_and(even, ~root))),
+        ((0, 0), far_to_root),
+        (at(-9), jnp.logical_and(z == 4, even)),
+        (at(4), jnp.logical_and(z == 3, even)),
+    )
+    end = jnp.logical_and(last, odd)
+    far_greeted = jnp.where(
+        jnp.logical_or(jnp.logical_or(z == 3, end), jnp.logical_or(z == 5, z == 6)), 1, 0
+    )
+    far_greeted = jnp.where(far_to_root, 0, jnp.where(root, 2, far_greeted))
     barrier = pltpu.get_barrier_semaphore()
-    for device, when in greets:
+    for device, when in greets + far_greets:
 
         @pl.when(when)
         def _():
             pl.semaphore_signal(barrier, inc=1, device_id=device, device_id_type=MESH)
 
-    here_first = sum(jnp.where(when, 1, 0) for _, when in greeted)
+    here_first = sum(jnp.where(when, 1, 0) for _, when in greeted) + far_greeted
 
     @pl.when(here_first > 0)
     def _():
@@ -104,6 +138,21 @@
             pl.semaphore_signal(
                 ready_sem.at[mirror[n]], inc=1, device_id=device, device_id_type=MESH
             )
+
+    for device in (at(-9), at(-10)):
+
+        @pl.when(root)
+        def _():
+            pl.semaphore_signal(ready_sem.at[6], inc=1, device_id=device, device_id_type=MESH)
+
+    @pl.when(end)
+    def _():
+        pl.semaphore_signal(ready_sem.at[6], inc=1, device_id=at(9), device_id_type=MESH)
+
+    def far_ready():
+        @pl.when(jnp.logical_or(far_to_root, jnp.logical_and(z == 4, even)))
+        def _():
+            pl.semaphore_wait(ready_sem.at[6], 1)
 
     def ready(n, when):
         @pl.when(jnp.logical_and(greets[n][1], when))
@@ -138,7 +187,7 @@
         ).wait_recv()
 
     def part(k):
-        return pl.ds(k * piece, piece)
+        return pl.ds(pl.multiple_of(k * piece, piece), piece)
 
     def lane(s, hop, k, core):
         start = pl.multiple_of(core * rows + k * piece, piece)
@@ -148,19 +197,32 @@
         for k in range(CHUNKS):
             send(source[s].at[part(k)], lane(s, 0, k, c), hop_sem.at[s, 0, k], along[s], when)
 
-    def send_cross(when):
-        for s in range(2):
-            send(source[s], cross.at[s], cross_sem.at[s], over[s], when)
-
-    send_own(1, inner_down)
-    send(images, ext.at[1], ext_sem.at[1], nextdoor[1], c == 1)
-    ready(0, inner_up)
+    def send_cross(s, when):
+        ready(4 + s, when)
+        send(source[s], cross.at[s], cross_sem.at[s], over[s], when)
+
+    def send_far(width, db, when, block=texts):
+        for k in range(CHUNKS):
+            dst, recv = width(k)
+            send(block.at[part(k)], dst, recv, at(db), when)
+
+    below_root = is_root(along[1])
+    late = jnp.logical_or(first, below_root)
+    send_far(lambda k: (lane(0, 2, k, c), hop_sem.at[0, 2, k]), 6, jnp.logical_and(z == 5, odd))
+    send_far(lambda k: (lane(0, 1, k, c), hop_sem.at[0, 1, k]), 4, z == 6)
+    send_own(1, ~late)
+    ready(0, g >= 0)
     send_own(0, g >= 0)
-    ready(2, c == 0)
-    send(texts, ext.at[0], ext_sem.at[0], nextdoor[0], c == 0)
-    ready(4, g >= 0)
-    ready(5, g >= 0)
-    send_cross(inner_up)
+    send_far(lambda k: (relay.at[part(k)], relay_sem.at[k]), -4, jnp.logical_and(z == 5, even))
+    send_far(lambda k: (relay.at[part(k)], relay_sem.at[k]), -2, jnp.logical_and(z == 4, odd))
+    send_far(
+        lambda k: (relay.at[part(k)], relay_sem.at[k]), 2, jnp.logical_and(z == 3, even), images
+    )
+    send(images, ext.at[1], ext_sem.at[1], nextdoor[1], jnp.logical_and(odd, ~first))
+    ready(2, even)
+    send(texts, ext.at[0], ext_sem.at[0], nextdoor[0], even)
+    for s in range(2):
+        send_cross(s, jnp.logical_and(inner_up, ~is_root(over[s])))
 
     def meet(side, block, positive=False, first=False):
         values = block[...]
@@ -205,13 +267,21 @@
             def _(s):
                 meet(s, cross.at[s])
 
-    ready(2, c == 1)
-    meet_cross(first)
-    ready(1, first)
-    ready(3, first)
-    send_own(1, first)
-
-    code = jnp.where(first, 19, jnp.where(z == 1, 22, jnp.where(last, 50, 42)))
+    ready(2, odd)
+    ready(1, late)
+    send_own(1, late)
+    ready(3, g >= 0)
+    send(images, ext.at[1], ext_sem.at[1], nextdoor[1], jnp.logical_and(odd, first))
+    for s in range(2):
+        send_cross(s, jnp.logical_and(inner_up, is_root(over[s])))
+
+    by_root = jnp.logical_and(b < 16, g == 0)
+    code = jnp.where(jnp.logical_or(first, last), 19, jnp.where(z == 1, 14, jnp.where(z == 2, 26, 42)))
+    code = jnp.where(
+        jnp.logical_and(by_root, z == 1),
+        19,
+        jnp.where(jnp.logical_and(by_root, z == 2), 22, jnp.where(jnp.logical_and(by_root, z == 3), 26, code)),
+    )
 
     def stream_hop(i):
         s = lax.rem(code // (1 << i), 2)
@@ -220,43 +290,83 @@
 
     steps = [stream_hop(i) for i in range(2 * HOPS)]
 
+    def stays(s):
+        return jnp.logical_or(inner_up, s == 1)
+
+    def ends(s):
+        return jnp.logical_or(inner_down, s == 0)
+
+    def pass_relay():
+        for k in range(CHUNKS):
+            here = relay.at[part(k)]
+            relays = jnp.logical_or(z == 3, jnp.logical_and(z == 4, even))
+
+            @pl.when(relays)
+            def _():
+                arrived(here, relay_sem.at[k])
+
+            send(here, lane(0, 2, k, c), hop_sem.at[0, 2, k], at(10), jnp.logical_and(z == 3, even))
+            send(here, ext.at[0, part(k)], late_sem(ext_sem, 0, k), at(9), jnp.logical_and(z == 3, odd))
+            send(here, ext.at[1, part(k)], late_sem(ext_sem, 1, k), at(-9), jnp.logical_and(z == 4, even))
+
+    def stage(i, k):
+        mix = {2: first, 3: first, 4: z == 1, 5: z == 1}.get(i)
+        if mix is None:
+            return (*steps[i], k)
+        base = i - i % 2
+        j = (i - base) * CHUNKS + k
+        (s0, h0), (s1, h1) = steps[base], steps[base + 1]
+        pick = jnp.where(mix, j % 2, i - base)
+        return (
+            jnp.where(pick == 0, s0, s1),
+            jnp.where(pick == 0, h0, h1),
+            jnp.where(mix, j // 2, k),
+        )
+
     def forwards(i, k):
-        s, hop = steps[i]
+        n = i * CHUNKS + k
+        s, hop, k = stage(i, k)
         here = lane(s, hop, k, c)
         further = lane(s, lax.rem(hop + 1, HOPS), k, c)
-        n = i * CHUNKS + k
         return (
             (
                 copy_to(here, further, hop_sem.at[s, lax.rem(hop + 1, HOPS), k], at(2 - 4 * s), hop_send.at[n, 0]),
-                hop + 1 < HOPS,
+                jnp.logical_and(hop + 1 < HOPS, stays(s)),
             ),
             (
                 copy_to(here, ext.at[s, part(k)], late_sem(ext_sem, s, k), at(1 - 2 * s), hop_send.at[n, 0]),
-                jnp.logical_and(hop + 1 == HOPS, c == 1 - s),
+                jnp.logical_and(
+                    jnp.logical_and(hop + 1 == HOPS, c == 1 - s), jnp.logical_and(stays(s), ends(s))
+                ),
             ),
             (copy_to(here, here, sib_sem.at[s, hop, k], sib, hop_send.at[n, 1]), g >= 0),
         )
 
     for i in range(2 * HOPS + 1):
         if i < 2 * HOPS:
-            s, hop = steps[i]
             for k in range(CHUNKS):
-                arrived(lane(s, hop, k, c), hop_sem.at[s, hop, k])
+                s, hop, p = stage(i, k)
+                arrived(lane(s, hop, p, c), hop_sem.at[s, hop, p])
                 for copy, when in forwards(i, k):
                     pl.when(when)(copy.start)
+        if i == RELAY_AT:
+            far_ready()
+            pass_relay()
+        if i == CROSS_AT:
+            for s in range(2):
+                send_cross(s, last)
         if i == 1:
             early = 1 - c
             arrived(ext.at[early], ext_sem.at[early])
             meet(early, ext.at[early])
         if i == 3:
             meet_cross(jnp.logical_and(inner_up, inner_down))
-            send_cross(last)
         if i >= 1:
             s, hop = steps[i - 1]
             for k in range(CHUNKS):
                 arrived(lane(s, hop, k, 1 - c), sib_sem.at[s, hop, k])
             meet(s, pair.at[s, hop])
-    meet_cross(last)
+    meet_cross(jnp.logical_or(first, last))
     for k in range(CHUNKS):
         arrived(ext.at[c, part(k)], late_sem(ext_sem, c, k))
     meet(c, ext.at[c])
@@ -316,13 +426,15 @@
                 pltpu.VMEM((2, rows, width), f32),
                 pltpu.VMEM((2, rows, rows), f32),
                 pltpu.SemaphoreType.DMA((4,)),
-                pltpu.SemaphoreType.DMA((3 * CHUNKS + 6,)),
+                pltpu.VMEM((rows, width), bf16),
+                pltpu.SemaphoreType.DMA((CHUNKS,)),
+                pltpu.SemaphoreType.DMA((11 * CHUNKS + 9,)),
                 pltpu.SemaphoreType.DMA((2 * HOPS * CHUNKS, 2)),
                 pltpu.SemaphoreType.DMA((2, HOPS, CHUNKS)),
                 pltpu.SemaphoreType.DMA((2, HOPS, CHUNKS)),
                 pltpu.SemaphoreType.DMA((2 + 2 * CHUNKS,)),
                 pltpu.SemaphoreType.DMA((2,)),
-                pltpu.SemaphoreType.REGULAR((6,)),
+                pltpu.SemaphoreType.REGULAR((7,)),
                 pltpu.SMEM((1,), f32),
                 pltpu.SMEM((1,), f32),
             ],

time: 61.4 us -> 56.6 us (0.922)
  Pallas kernels: 57.1 us -> 52.5 us
    pallas_call x1, Pallas kernels: 56.1 us -> 51.4 us  [on_device(): pl.pallas_call(functools.partial(kernel, n_blk, n_grp), out_shape=(jax.Sh...]
where the time goes in v2:
time: 56.6 us; the launch traced here: 56.4 us
  Pallas kernels  52.5 us (93%)
  between operations  1.94 us (3%)
  local copies, waits for them, and re-layouts  1.92 us (3%)
    pallas_call x1, Pallas kernels, on_device(): pl.pallas_call(functools.partial(kernel, n_blk, n_grp), out_shape=(jax.Sh...  51.4 us
    unnamed x4, local copies, waits for them, and re-layouts  1.92 us

profile of v2, /device:TPU:1, one launch (start us, length us, event | category | flops | bytes accessed | tf_op | source)
XLA Modules:
  0.0 56.4 jit_solution(9176832220970515730)
XLA Ops:
  1.9 0.0 copy-start
  1.9 1.0 %copy-done = bf16[128,1152]{1,0:T(8,128)(2,1)S(1)} copy-done((bf16[128,1152]{1,0:T(8,128)(2,1)S(1)}, bf16[128,1152]{1,0:T(8,128)(2,1)}, u32[]{:S(2)}) %copy-start) | copy-done | bytes 294936
  2.9 0.0 copy-start.1
  2.9 1.0 %copy-done.1 = bf16[128,1152]{1,0:T(8,128)(2,1)S(1)} copy-done((bf16[128,1152]{1,0:T(8,128)(2,1)S(1)}, bf16[128,1152]{1,0:T(8,128)(2,1)}, u32[]{:S(2)}) %copy-start.1) | copy-done | bytes 294936
  3.8 51.4 %shard_map.67 = (f32[1,128]{1,0:T(1,128)S(1)}, f32[2,128,1152]{2,1,0:T(8,128)S(1)}) custom-call(bf16[128,1152]{1,0:T(8,128)(2,1)S(1)} %copy-done, bf16[128,1152]{1,0:T(8,128)(2,1)S(1)} %copy-done.1, f32[1]{0:T(128)S(6)} %copy.7.scale_in, f32[1]{0:T(128)S(6)} %copy.8.bias_in), custom_call_target="tpu_custom_call" | custom-call | tf_op jit(solution)/shard_map/pallas_call | solution.py:413
  55.3 1.1 %shard_map.68 = (f32[1,128]{1,0:T(1,128)}, f32[128,1152]{1,0:T(8,128)}, f32[128,1152]{1,0:T(8,128)}) custom-call(f32[1,128]{1,0:T(1,128)S(1)} %get-tuple-element.8.loss_in, f32[2,128,1152]{2,1,0:T(8,128)S(1)} %get-tuple-element.9.grad_in), custom_call_target="tpu_custom_call" | custom-call | tf_op jit(solution)/shard_map/pallas_call | solution.py:445
Async XLA Ops:
  1.9 1.0 %copy-start = (bf16[128,1152]{1,0:T(8,128)(2,1)S(1)}, bf16[128,1152]{1,0:T(8,128)(2,1)}, u32[]{:S(2)}) copy-start(bf16[128,1152]{1,0:T(8,128)(2,1)} %images.1) | copy-start | bytes 884740
  2.9 1.0 %copy-start.1 = (bf16[128,1152]{1,0:T(8,128)(2,1)S(1)}, bf16[128,1152]{1,0:T(8,128)(2,1)}, u32[]{:S(2)}) copy-start(bf16[128,1152]{1,0:T(8,128)(2,1)} %texts.1) | copy-start | bytes 884740

commit v3 on v2

--- a/solution.py
+++ b/solution.py
@@ -8,9 +8,10 @@
 from jax.sharding import PartitionSpec as P
 
 HOPS = 3
-CHUNKS = 4
+CHUNKS = 2
 RELAY_AT = 2
-CROSS_AT = 0
+FAR_AT = 0
+CROSS_AT = 1
 VMEM_LIMIT = 48 * 2**20
 MESH = pl.DeviceIdType.MESH
 
@@ -207,65 +208,72 @@
             send(block.at[part(k)], dst, recv, at(db), when)
 
     below_root = is_root(along[1])
+    cross_late = z >= 5
     late = jnp.logical_or(first, below_root)
     send_far(lambda k: (lane(0, 2, k, c), hop_sem.at[0, 2, k]), 6, jnp.logical_and(z == 5, odd))
-    send_far(lambda k: (lane(0, 1, k, c), hop_sem.at[0, 1, k]), 4, z == 6)
     send_own(1, ~late)
     ready(0, g >= 0)
     send_own(0, g >= 0)
     send_far(lambda k: (relay.at[part(k)], relay_sem.at[k]), -4, jnp.logical_and(z == 5, even))
     send_far(lambda k: (relay.at[part(k)], relay_sem.at[k]), -2, jnp.logical_and(z == 4, odd))
-    send_far(
-        lambda k: (relay.at[part(k)], relay_sem.at[k]), 2, jnp.logical_and(z == 3, even), images
-    )
     send(images, ext.at[1], ext_sem.at[1], nextdoor[1], jnp.logical_and(odd, ~first))
     ready(2, even)
     send(texts, ext.at[0], ext_sem.at[0], nextdoor[0], even)
     for s in range(2):
-        send_cross(s, jnp.logical_and(inner_up, ~is_root(over[s])))
-
-    def meet(side, block, positive=False, first=False):
-        values = block[...]
-        dots = lax.dot_general(
-            own[side], values, (((1,), (1,)), ((), ())), preferred_element_type=jnp.float32
-        )
-        score = factor * dots + offset
-        if positive:
-            diagonal = lax.broadcasted_iota(jnp.int32, score.shape, 0) == lax.broadcasted_iota(
-                jnp.int32, score.shape, 1
+        send_cross(s, jnp.logical_and(~cross_late, ~is_root(over[s])))
+
+    def meet(pairs, positive=False):
+        values = [block[...] for _, block in pairs]
+        scores = [
+            factor
+            * lax.dot_general(
+                own[side], value, (((1,), (1,)), ((), ())), preferred_element_type=jnp.float32
             )
-            score = jnp.where(diagonal, -score, score)
-        small = jnp.exp(-jnp.abs(score))
-        share = 1.0 / (1.0 + small)
-        coef = jnp.where(score >= 0, share, small * share)
-        if positive:
-            coef = jnp.where(diagonal, -coef, coef)
-        term = jnp.maximum(score, 0.0) + jnp.log1p(small)
-        if score.shape[1] > rows:
-            term = term[:, :rows] + term[:, rows:]
-        grad = jnp.dot(coef.astype(jnp.bfloat16), values, preferred_element_type=jnp.float32)
-        if first:
-            lacc[side] = term
-            acc[side] = grad
-        else:
-            lacc[side] += term
-            acc[side] += grad
+            + offset
+            for (side, _), value in zip(pairs, values)
+        ]
+        coefs, terms = [], []
+        for score in scores:
+            if positive:
+                diagonal = lax.broadcasted_iota(jnp.int32, score.shape, 0) == lax.broadcasted_iota(
+                    jnp.int32, score.shape, 1
+                )
+                score = jnp.where(diagonal, -score, score)
+            small = jnp.exp(-jnp.abs(score))
+            share = 1.0 / (1.0 + small)
+            coef = jnp.where(score >= 0, share, small * share)
+            if positive:
+                coef = jnp.where(diagonal, -coef, coef)
+            term = jnp.maximum(score, 0.0) + jnp.log1p(small)
+            if score.shape[1] > rows:
+                term = term[:, :rows] + term[:, rows:]
+            coefs.append(coef.astype(jnp.bfloat16))
+            terms.append(term)
+        grads = [
+            jnp.dot(coef, value, preferred_element_type=jnp.float32)
+            for coef, value in zip(coefs, values)
+        ]
+        for (side, _), term, grad in zip(pairs, terms, grads):
+            if positive:
+                lacc[side] = term
+                acc[side] = grad
+            else:
+                lacc[side] += term
+                acc[side] += grad
 
     for load in loads:
         load.wait()
     factor, offset = scale[0], bias[0]
-    for side in range(2):
-        meet(side, own.at[1 - side], positive=True, first=True)
+    meet([(side, own.at[1 - side]) for side in range(2)], positive=True)
 
     def meet_cross(when):
         @pl.when(when)
         def _():
             for s in range(2):
                 arrived(cross.at[s], cross_sem.at[s])
-
-            @pl.loop(0, 2)
-            def _(s):
-                meet(s, cross.at[s])
+            early = 1 - c
+            arrived(ext.at[early], ext_sem.at[early])
+            meet([(0, cross.at[0]), (1, cross.at[1]), (early, ext.at[early])])
 
     ready(2, odd)
     ready(1, late)
@@ -273,10 +281,14 @@
     ready(3, g >= 0)
     send(images, ext.at[1], ext_sem.at[1], nextdoor[1], jnp.logical_and(odd, first))
     for s in range(2):
-        send_cross(s, jnp.logical_and(inner_up, is_root(over[s])))
+        send_cross(s, jnp.logical_and(~cross_late, is_root(over[s])))
 
     by_root = jnp.logical_and(b < 16, g == 0)
-    code = jnp.where(jnp.logical_or(first, last), 19, jnp.where(z == 1, 14, jnp.where(z == 2, 26, 42)))
+    code = jnp.where(
+        first,
+        jnp.where(even, 19, 35),
+        jnp.where(last, 19, jnp.where(z == 1, jnp.where(even, 14, 38), jnp.where(even, 26, 42))),
+    )
     code = jnp.where(
         jnp.logical_and(by_root, z == 1),
         19,
@@ -296,21 +308,21 @@
     def ends(s):
         return jnp.logical_or(inner_down, s == 0)
 
-    def pass_relay():
+    def pass_relay(when):
         for k in range(CHUNKS):
             here = relay.at[part(k)]
-            relays = jnp.logical_or(z == 3, jnp.logical_and(z == 4, even))
+            relays = jnp.logical_and(when, jnp.logical_or(z == 3, even))
 
             @pl.when(relays)
             def _():
                 arrived(here, relay_sem.at[k])
 
-            send(here, lane(0, 2, k, c), hop_sem.at[0, 2, k], at(10), jnp.logical_and(z == 3, even))
-            send(here, ext.at[0, part(k)], late_sem(ext_sem, 0, k), at(9), jnp.logical_and(z == 3, odd))
-            send(here, ext.at[1, part(k)], late_sem(ext_sem, 1, k), at(-9), jnp.logical_and(z == 4, even))
+            send(here, lane(0, 2, k, c), hop_sem.at[0, 2, k], at(10), jnp.logical_and(jnp.logical_and(when, z == 3), even))
+            send(here, ext.at[0, part(k)], late_sem(ext_sem, 0, k), at(9), jnp.logical_and(jnp.logical_and(when, z == 3), odd))
+            send(here, ext.at[1, part(k)], late_sem(ext_sem, 1, k), at(-9), jnp.logical_and(jnp.logical_and(when, z == 4), even))
 
     def stage(i, k):
-        mix = {2: first, 3: first, 4: z == 1, 5: z == 1}.get(i)
+        mix = None
         if mix is None:
             return (*steps[i], k)
         base = i - i % 2
@@ -347,29 +359,32 @@
             for k in range(CHUNKS):
                 s, hop, p = stage(i, k)
                 arrived(lane(s, hop, p, c), hop_sem.at[s, hop, p])
+                if i == 0 and k == 0:
+                    send_far(lambda k: (lane(0, 1, k, c), hop_sem.at[0, 1, k]), 4, z == 6)
                 for copy, when in forwards(i, k):
                     pl.when(when)(copy.start)
         if i == RELAY_AT:
+            send_far(
+                lambda k: (relay.at[part(k)], relay_sem.at[k]), 2, jnp.logical_and(z == 3, even), images
+            )
             far_ready()
-            pass_relay()
+            pass_relay(z == 3)
+        if i == RELAY_AT + 2:
+            pass_relay(z == 4)
         if i == CROSS_AT:
             for s in range(2):
-                send_cross(s, last)
-        if i == 1:
-            early = 1 - c
-            arrived(ext.at[early], ext_sem.at[early])
-            meet(early, ext.at[early])
+                send_cross(s, cross_late)
         if i == 3:
-            meet_cross(jnp.logical_and(inner_up, inner_down))
-        if i >= 1:
-            s, hop = steps[i - 1]
-            for k in range(CHUNKS):
-                arrived(lane(s, hop, k, 1 - c), sib_sem.at[s, hop, k])
-            meet(s, pair.at[s, hop])
-    meet_cross(jnp.logical_or(first, last))
+            meet_cross(jnp.logical_and(~cross_late, inner_down))
+        if i in (2, 4, 6):
+            for s, hop in steps[i - 2 : i]:
+                for k in range(CHUNKS):
+                    arrived(lane(s, hop, k, 1 - c), sib_sem.at[s, hop, k])
+            meet([(s, pair.at[s, hop]) for s, hop in steps[i - 2 : i]])
+    meet_cross(jnp.logical_or(first, cross_late))
     for k in range(CHUNKS):
         arrived(ext.at[c, part(k)], late_sem(ext_sem, c, k))
-    meet(c, ext.at[c])
+    meet([(c, ext.at[c])])
 
     for side in range(2):
         grad_out[side] = factor * acc[side]
@@ -416,7 +431,7 @@
                 jax.ShapeDtypeStruct((1, rows), f32),
                 jax.ShapeDtypeStruct((2, rows, width), f32),
             ),
-            in_specs=[hbm] * 4,
+            in_specs=[vmem, vmem, hbm, hbm],
             out_specs=(vmem, vmem),
             scratch_shapes=[
                 pltpu.VMEM((2, rows, width), bf16),
@@ -428,7 +443,7 @@
                 pltpu.SemaphoreType.DMA((4,)),
                 pltpu.VMEM((rows, width), bf16),
                 pltpu.SemaphoreType.DMA((CHUNKS,)),
-                pltpu.SemaphoreType.DMA((11 * CHUNKS + 9,)),
+                pltpu.SemaphoreType.DMA((14 * CHUNKS + 9,)),
                 pltpu.SemaphoreType.DMA((2 * HOPS * CHUNKS, 2)),
                 pltpu.SemaphoreType.DMA((2, HOPS, CHUNKS)),
                 pltpu.SemaphoreType.DMA((2, HOPS, CHUNKS)),

time: 56.6 us -> 53.2 us (0.940)
  the two profiles are of different devices: /device:TPU:1 before, /device:TPU:241 now
where the time goes in v3:
time: 53.2 us; the launch traced here: 53 us
  Pallas kernels  49.1 us (92%)
  between operations  1.94 us (4%)
  local copies, waits for them, and re-layouts  1.92 us (4%)
    pallas_call x1, Pallas kernels, on_device(): pl.pallas_call(functools.partial(kernel, n_blk, n_grp), out_shape=(jax.Sh...  48.1 us
    unnamed x4, local copies, waits for them, and re-layouts  1.92 us

profile of v3, /device:TPU:241, one launch (start us, length us, event | category | flops | bytes accessed | tf_op | source)
XLA Modules:
  0.0 53.0 jit_solution(3538771792437313574)
XLA Ops:
  1.9 0.0 copy-start
  1.9 1.0 %copy-done = bf16[128,1152]{1,0:T(8,128)(2,1)S(1)} copy-done((bf16[128,1152]{1,0:T(8,128)(2,1)S(1)}, bf16[128,1152]{1,0:T(8,128)(2,1)}, u32[]{:S(2)}) %copy-start) | copy-done | bytes 294936
  2.9 0.0 copy-start.1
  2.9 1.0 %copy-done.1 = bf16[128,1152]{1,0:T(8,128)(2,1)S(1)} copy-done((bf16[128,1152]{1,0:T(8,128)(2,1)S(1)}, bf16[128,1152]{1,0:T(8,128)(2,1)}, u32[]{:S(2)}) %copy-start.1) | copy-done | bytes 294936
  3.8 48.1 %shard_map.67 = (f32[1,128]{1,0:T(1,128)S(1)}, f32[2,128,1152]{2,1,0:T(8,128)S(1)}) custom-call(bf16[128,1152]{1,0:T(8,128)(2,1)S(1)} %copy-done, bf16[128,1152]{1,0:T(8,128)(2,1)S(1)} %copy-done.1, f32[1]{0:T(128)S(6)} %copy.7.scale_in, f32[1]{0:T(128)S(6)} %copy.8.bias_in), custom_call_target="tpu_custom_call" | custom-call | tf_op jit(solution)/shard_map/pallas_call | solution.py:428
  51.9 1.1 %shard_map.68 = (f32[1,128]{1,0:T(1,128)}, f32[128,1152]{1,0:T(8,128)}, f32[128,1152]{1,0:T(8,128)}) custom-call(f32[1,128]{1,0:T(1,128)S(1)} %get-tuple-element.8.loss_in, f32[2,128,1152]{2,1,0:T(8,128)S(1)} %get-tuple-element.9.grad_in), custom_call_target="tpu_custom_call" | custom-call | tf_op jit(solution)/shard_map/pallas_call | solution.py:460
Async XLA Ops:
  1.9 1.0 %copy-start = (bf16[128,1152]{1,0:T(8,128)(2,1)S(1)}, bf16[128,1152]{1,0:T(8,128)(2,1)}, u32[]{:S(2)}) copy-start(bf16[128,1152]{1,0:T(8,128)(2,1)} %images.1) | copy-start | bytes 884740
  2.9 1.0 %copy-start.1 = (bf16[128,1152]{1,0:T(8,128)(2,1)S(1)}, bf16[128,1152]{1,0:T(8,128)(2,1)}, u32[]{:S(2)}) copy-start(bf16[128,1152]{1,0:T(8,128)(2,1)} %texts.1) | copy-start | bytes 884740

commit v4 on v3

--- a/solution.py
+++ b/solution.py
@@ -11,7 +11,7 @@
 CHUNKS = 2
 RELAY_AT = 2
 FAR_AT = 0
-CROSS_AT = 1
+CROSS_AT = 2
 VMEM_LIMIT = 48 * 2**20
 MESH = pl.DeviceIdType.MESH
 
@@ -19,13 +19,11 @@
 def kernel(
     n_blk,
     n_grp,
-    images,
-    texts,
+    own,
     scale_in,
     bias_in,
     loss_out,
     grad_out,
-    own,
     pair,
     ext,
     cross,
@@ -62,13 +60,12 @@
     along2 = (at(4), at(-4))
     nextdoor = (at(1), at(-1))
     over = (at(0, 1), at(0, -1))
+    images, texts = own.at[0], own.at[1]
     source = (texts, images)
 
     loads = [
-        pltpu.make_async_copy(images, own.at[0], load_sem.at[0]),
-        pltpu.make_async_copy(texts, own.at[1], load_sem.at[1]),
-        pltpu.make_async_copy(scale_in, scale, load_sem.at[2]),
-        pltpu.make_async_copy(bias_in, bias, load_sem.at[3]),
+        pltpu.make_async_copy(scale_in, scale, load_sem.at[0]),
+        pltpu.make_async_copy(bias_in, bias, load_sem.at[1]),
     ]
     for load in loads:
         load.start()
@@ -431,16 +428,15 @@
                 jax.ShapeDtypeStruct((1, rows), f32),
                 jax.ShapeDtypeStruct((2, rows, width), f32),
             ),
-            in_specs=[vmem, vmem, hbm, hbm],
+            in_specs=[vmem, hbm, hbm],
             out_specs=(vmem, vmem),
             scratch_shapes=[
-                pltpu.VMEM((2, rows, width), bf16),
                 pltpu.VMEM((2, HOPS, 2 * rows, width), bf16),
                 pltpu.VMEM((2, rows, width), bf16),
                 pltpu.VMEM((2, rows, width), bf16),
                 pltpu.VMEM((2, rows, width), f32),
                 pltpu.VMEM((2, rows, rows), f32),
-                pltpu.SemaphoreType.DMA((4,)),
+                pltpu.SemaphoreType.DMA((2,)),
                 pltpu.VMEM((rows, width), bf16),
                 pltpu.SemaphoreType.DMA((CHUNKS,)),
                 pltpu.SemaphoreType.DMA((14 * CHUNKS + 9,)),
@@ -456,7 +452,7 @@
             compiler_params=pltpu.CompilerParams(
                 collective_id=0, has_side_effects=True, vmem_limit_bytes=VMEM_LIMIT
             ),
-        )(images, texts, scale, bias)
+        )(jnp.stack((images, texts)), scale, bias)
         loss, gimg, gtxt = pl.pallas_call(
             hand_over,
             out_shape=(

time: 53.2 us -> 51.4 us (0.966)
  the two profiles are of different devices: /device:TPU:241 before, /device:TPU:1 now
where the time goes in v4:
time: 51.4 us; the launch traced here: 51.2 us
  Pallas kernels  48.1 us (94%)
  between operations  1.93 us (4%)
  other arithmetic  1.11 us (2%)
    pallas_call x1, Pallas kernels, on_device(): pl.pallas_call(functools.partial(kernel, n_blk, n_grp), out_shape=(jax.Sh...  47.1 us
    another operation x1, other arithmetic, on_device(): jnp.stack((images, texts))  1.11 us
    pallas_call x1, Pallas kernels, on_device(): pl.pallas_call(hand_over, out_shape=(jax.ShapeDtypeStruct((1, rows), f32)...  1.06 us

profile of v4, /device:TPU:1, one launch (start us, length us, event | category | flops | bytes accessed | tf_op | source)
XLA Modules:
  0.0 51.2 jit_solution(10277962498205085559)
XLA Ops:
  1.9 1.1 %pad_maximum_fusion.own = bf16[2,128,1152]{2,1,0:T(8,128)(2,1)S(1)} fusion(bf16[1,128,1152]{2,1,0:T(8,128)(2,1)} %bitcast.3, bf16[1,128,1152]{2,1,0:T(8,128)(2,1)} %bitcast.4), kind=kLoop, calls=%fused_computation | loop fusion | flops 294912 | bytes 1179648 | tf_op jit(solution)/shard_map/stack | solution.py:455
  3.0 47.1 %shard_map.67 = (f32[1,128]{1,0:T(1,128)S(1)}, f32[2,128,1152]{2,1,0:T(8,128)S(1)}) custom-call(bf16[2,128,1152]{2,1,0:T(8,128)(2,1)S(1)} %pad_maximum_fusion.own, f32[1]{0:T(128)S(6)} %copy.7.scale_in, f32[1]{0:T(128)S(6)} %copy.8.bias_in), custom_call_target="tpu_custom_call" | custom-call | tf_op jit(solution)/shard_map/pallas_call | solution.py:425
  50.1 1.1 %shard_map.68 = (f32[1,128]{1,0:T(1,128)}, f32[128,1152]{1,0:T(8,128)}, f32[128,1152]{1,0:T(8,128)}) custom-call(f32[1,128]{1,0:T(1,128)S(1)} %get-tuple-element.8.loss_in, f32[2,128,1152]{2,1,0:T(8,128)S(1)} %get-tuple-element.9.grad_in), custom_call_target="tpu_custom_call" | custom-call | tf_op jit(solution)/shard_map/pallas_call | solution.py:456

commit v5 on v4

--- a/solution.py
+++ b/solution.py
@@ -8,7 +8,7 @@
 from jax.sharding import PartitionSpec as P
 
 HOPS = 3
-CHUNKS = 2
+CHUNKS = 4
 RELAY_AT = 2
 FAR_AT = 0
 CROSS_AT = 2

time: 51.4 us -> 51.4 us (level)
  no operation moved by 1% of the time
where the time goes in v5:
time: 51.4 us; the launch traced here: 51.2 us
  Pallas kernels  48.2 us (94%)
  between operations  1.93 us (4%)
  other arithmetic  1.11 us (2%)
    pallas_call x1, Pallas kernels, on_device(): pl.pallas_call(functools.partial(kernel, n_blk, n_grp), out_shape=(jax.Sh...  47.1 us
    another operation x1, other arithmetic, on_device(): jnp.stack((images, texts))  1.11 us
    pallas_call x1, Pallas kernels, on_device(): pl.pallas_call(hand_over, out_shape=(jax.ShapeDtypeStruct((1, rows), f32)...  1.06 us

profile of v5, /device:TPU:1, one launch (start us, length us, event | category | flops | bytes accessed | tf_op | source)
XLA Modules:
  0.0 51.2 jit_solution(2134294125524873910)
XLA Ops:
  1.9 1.1 %pad_maximum_fusion.own = bf16[2,128,1152]{2,1,0:T(8,128)(2,1)S(1)} fusion(bf16[1,128,1152]{2,1,0:T(8,128)(2,1)} %bitcast.3, bf16[1,128,1152]{2,1,0:T(8,128)(2,1)} %bitcast.4), kind=kLoop, calls=%fused_computation | loop fusion | flops 294912 | bytes 1179648 | tf_op jit(solution)/shard_map/stack | solution.py:455
  3.0 47.1 %shard_map.67 = (f32[1,128]{1,0:T(1,128)S(1)}, f32[2,128,1152]{2,1,0:T(8,128)S(1)}) custom-call(bf16[2,128,1152]{2,1,0:T(8,128)(2,1)S(1)} %pad_maximum_fusion.own, f32[1]{0:T(128)S(6)} %copy.7.scale_in, f32[1]{0:T(128)S(6)} %copy.8.bias_in), custom_call_target="tpu_custom_call" | custom-call | tf_op jit(solution)/shard_map/pallas_call | solution.py:425
  50.2 1.1 %shard_map.68 = (f32[1,128]{1,0:T(1,128)}, f32[128,1152]{1,0:T(8,128)}, f32[128,1152]{1,0:T(8,128)}) custom-call(f32[1,128]{1,0:T(1,128)S(1)} %get-tuple-element.8.loss_in, f32[2,128,1152]{2,1,0:T(8,128)S(1)} %get-tuple-element.9.grad_in), custom_call_target="tpu_custom_call" | custom-call | tf_op jit(solution)/shard_map/pallas_call | solution.py:456
